TPU v7x, 128 devices: a whole 4x4x4 slice. The times are simulated.
128 devices in a mesh: side: 2 (over core), wide: 16 (over z, y), narrow: 4 (over x).
Axes of the slice: x: 4, y: 4, z: 4, core: 2. Of those that a mesh axis runs over, the one named last changes fastest.
Arguments:
- queries: bfloat16 [64, 8192], P(('side', 'wide')), may hold values from -20 to 20
- key_cache: bfloat16 [64, 4096, 1024], P(('side', 'wide'), 'narrow'), may hold values from -20 to 20
- value_cache: bfloat16 [64, 4096, 1024], P(('side', 'wide'), 'narrow'), may hold values from -6 to 6
- latest_key: bfloat16 [64, 1024], P(('side', 'wide')), may hold values from -20 to 20
- latest_value: bfloat16 [64, 1024], P(('side', 'wide')), may hold values from -6 to 6
- lengths: int32 [64], P(('side', 'wide')), may hold values from 1 to 4096, 131072 in all
- residual: bfloat16 [64, 8192], P(None, ('side', 'wide', 'narrow')), may hold values from -6 to 6
- o_weight: bfloat16 [8192, 8192], P(None, ('side', 'wide', 'narrow')), may hold values from -0.0625 to 0.0625
- norm_gain: bfloat16 [8192], P(('side', 'wide', 'narrow')), may hold values from 0.5 to 1.5
- gate_weight: bfloat16 [8192, 28672], P(None, ('side', 'wide', 'narrow')), may hold values from -0.0625 to 0.0625
- up_weight: bfloat16 [8192, 28672], P(None, ('side', 'wide', 'narrow')), may hold values from -0.0625 to 0.0625
- down_weight: bfloat16 [28672, 8192], P(('side', 'wide', 'narrow')), may hold values from -0.125 to 0.125
Outputs:
- layer_out: bfloat16 [64, 8192], P(None, ('side', 'wide', 'narrow'))
Inputs may be any that keep to these rules, and one draw needn't show every extreme that they name: `lengths`: some session has exactly 4096 valid positions.
All inputs are finite; a program needn't handle non-finite values. No bound on the sum of `lengths` on one device may be relied on, other than what follows from the above.
Results may differ from a plain program's by a relative error of at most 0.0152.
Values may be sent and summed in bfloat16 or wider, within the bound.
A program may use at most 64 MiB of HBM per device.

v0:
```python
import jax
import jax.numpy as jnp
from jax import lax
from jax.sharding import PartitionSpec as P

D = 8192
KEY_VALUE_HEADS = 8
HEAD_SIZE = 128


def combined_all(value, axis, join):
    pieces = jax.tree.map(lambda part: lax.all_gather(part, axis), value)
    head = jax.tree.map(lambda part: part[0], pieces)
    tail = jax.tree.map(lambda part: part[1:], pieces)
    running, _ = lax.scan(lambda running, section: (join(running, section), None), head, tail)
    return running


def join_partials(leading, second):
    peak = jnp.maximum(leading[0], second[0])
    first_scale = jnp.exp(leading[0] - peak)
    second_scale = jnp.exp(second[0] - peak)
    denominator = leading[1] * first_scale + second[1] * second_scale
    numerator = leading[2] * first_scale[..., None] + second[2] * second_scale[..., None]
    return (peak, denominator, numerator)


def on_device(
    queries,
    key_cache,
    value_cache,
    latest_key,
    latest_value,
    lengths,
    residual,
    o_weight,
    norm_gain,
    gate_weight,
    up_weight,
    down_weight,
):
    scaling = HEAD_SIZE ** (-0.5)
    session_list = queries.shape[0]
    portion_length = key_cache.shape[1]
    query_groups = queries.shape[1] // (KEY_VALUE_HEADS * HEAD_SIZE)
    query_lines = queries.reshape(session_list, KEY_VALUE_HEADS, query_groups, HEAD_SIZE)
    key_lines = key_cache.reshape(session_list, portion_length, KEY_VALUE_HEADS, HEAD_SIZE)
    value_lines = value_cache.reshape(session_list, portion_length, KEY_VALUE_HEADS, HEAD_SIZE)
    scores = (
        jnp.einsum("sgqd,stgd->sgqt", query_lines, key_lines, preferred_element_type=jnp.float32)
        * scaling
    )
    displacement = lax.axis_index("narrow") * portion_length
    positions = displacement + jnp.arange(portion_length, dtype=jnp.int32)
    valid = (positions[None, :] < lengths[:, None])[:, None, None, :]
    scores = jnp.where(valid, scores, jnp.float32(-1e30))
    largest = jnp.max(scores, axis=-1)
    weights = jnp.where(valid, jnp.exp(scores - largest[..., None]), jnp.float32(0.0))
    denominator = jnp.sum(weights, axis=-1)
    numerator = jnp.einsum(
        "sgqt,stgd->sgqd",
        weights.astype(jnp.bfloat16),
        value_lines,
        preferred_element_type=jnp.float32,
    )
    largest, denominator, numerator = combined_all(
        (largest, denominator, numerator), "narrow", join_partials
    )
    incoming_key = latest_key.reshape(session_list, KEY_VALUE_HEADS, HEAD_SIZE)
    incoming_value = latest_value.astype(jnp.float32).reshape(
        session_list, KEY_VALUE_HEADS, 1, HEAD_SIZE
    )
    new_score = (
        jnp.einsum("sgqd,sgd->sgq", query_lines, incoming_key, preferred_element_type=jnp.float32)
        * scaling
    )
    peak = jnp.maximum(largest, new_score)
    shrink = jnp.exp(largest - peak)
    own_term = jnp.exp(new_score - peak)
    attended = (numerator * shrink[..., None] + own_term[..., None] * incoming_value) / (
        denominator * shrink + own_term
    )[..., None]
    attended = attended.reshape(session_list, -1).astype(jnp.bfloat16)
    projected = jnp.dot(
        lax.all_gather(attended, ("side", "wide"), axis=0, tiled=True),
        o_weight,
        preferred_element_type=jnp.float32,
    )
    stream = (residual.astype(jnp.float32) + projected).astype(jnp.bfloat16)
    stream_f = stream.astype(jnp.float32)
    squares = lax.psum(jnp.sum(stream_f * stream_f, axis=-1), ("side", "wide", "narrow"))
    inverse = lax.rsqrt(squares / D + 1e-05)
    normed = (stream_f * inverse[:, None] * norm_gain.astype(jnp.float32)).astype(jnp.bfloat16)
    piece = lax.all_gather(normed, ("side", "wide", "narrow"), axis=1, tiled=True)
    gate_sum = jnp.dot(piece, gate_weight, preferred_element_type=jnp.float32)
    up_sum = jnp.dot(piece, up_weight, preferred_element_type=jnp.float32)
    hidden = (jax.nn.silu(gate_sum) * up_sum).astype(jnp.bfloat16)
    down_terms = jnp.dot(hidden, down_weight, preferred_element_type=jnp.float32)
    summed = lax.psum_scatter(
        down_terms, ("side", "wide", "narrow"), scatter_dimension=1, tiled=True
    )
    return (stream_f + summed).astype(jnp.bfloat16)


def solution(mesh):
    return jax.shard_map(
        on_device,
        mesh=mesh,
        in_specs=(
            P(("side", "wide"), None),
            P(("side", "wide"), "narrow", None),
            P(("side", "wide"), "narrow", None),
            P(("side", "wide"), None),
            P(("side", "wide"), None),
            P(("side", "wide")),
            P(None, ("side", "wide", "narrow")),
            P(None, ("side", "wide", "narrow")),
            P(("side", "wide", "narrow")),
            P(None, ("side", "wide", "narrow")),
            P(None, ("side", "wide", "narrow")),
            P(("side", "wide", "narrow"), None),
        ),
        out_specs=P(None, ("side", "wide", "narrow")),
        check_vma=False,
    )
```

profile of v0, /device:TPU:1, one launch (start us, length us, event | category | flops | bytes accessed | tf_op | source)
XLA Modules:
  0.0 904.2 jit_solution(17236982720480294495)
XLA Ops:
  6.5 0.0 copy-start
  6.5 0.0 all-gather.9.cloned.1.call-start
  6.5 0.0 copy-start.2
  6.5 0.9 broadcast_compare_fusion
  7.4 3.8 fusion.43
  11.2 0.0 copy-start.5
  11.2 0.0 copy-start.3
  11.2 0.0 copy-start.6
  11.2 10.3 %all-gather = f32[8,8,8]{2,1,0:T(8,128)S(1)} all-gather(f32[2,8,8]{2,1,0:T(8,128)S(1)} %get-tuple-element.68), channel_id=2, replica_groups=mesh['side'=2,'wide'=16,'narrow'=4] {'narrow'}, dimensions={0}, use_global_device_ids=true | all-gather | bytes 2560 | tf_op jit(solution)/shard_map/all_gather | solution.py:12
  21.5 0.2 fusion.20
  21.8 9.0 all-gather.1
  30.8 0.0 copy-done.2
  30.8 0.0 copy-start.7
  30.8 0.0 copy-start.4
  30.8 1.0 fusion.3
  31.8 9.6 %all-gather.2 = f32[8,8,8,128]{3,2,1,0:T(8,128)S(1)} all-gather(f32[2,8,8,128]{3,2,1,0:T(8,128)S(1)} %fusion.3), channel_id=4, replica_groups=mesh['side'=2,'wide'=16,'narrow'=4] {'narrow'}, dimensions={0}, use_global_device_ids=true | all-gather | bytes 327680 | tf_op jit(solution)/shard_map/all_gather | solution.py:12
  41.5 0.0 copy-done.5
  41.5 0.0 copy-done.3
  41.5 0.1 fusion.30
  41.6 0.0 copy-done.6
  41.7 0.5 while.14
  41.7 0.1 fusion.58
  41.9 0.1 fusion.58
  42.0 0.1 fusion.58
  42.2 0.1 divide_convert_fusion
  42.3 0.6 reshape.68
  42.9 0.0 all-gather.9.cloned.1.call-update
  42.9 0.0 all-gather.7.cloned.1.call-start
  43.0 0.0 copy-done.7
  43.0 0.0 copy-done.4
  43.0 0.1 copy.18
  43.1 53.5 %all-gather.9.cloned.1.call-done = bf16[32,2,8192]{2,1,0:T(2,128)(2,1)} async-done(((bf16[1,2,8192]{2,1,0:T(2,128)(2,1)}), bf16[32,2,8192]{2,1,0:T(2,128)(2,1)}) %all-gather.9.cloned.1.call-update) | async-done | bytes 1048592 | tf_op jit(solution)/shard_map/all_gather | solution.py:85
  96.6 1.5 reshape.69
  98.1 0.0 copy-done
  98.1 0.4 multiply_reduce_fusion
  98.5 64.1 %psum.7 = f32[64]{0:T(128)S(1)} all-reduce(f32[64]{0:T(128)S(1)} %get-tuple-element.70), channel_id=1, replica_groups=mesh['side'=2,'wide'=16,'narrow'=4] {'side','wide','narrow'}, use_global_device_ids=true, to_apply=%region_5.6 | all-reduce | flops 64 | bytes 512 | tf_op jit(solution)/shard_map/psum | solution.py:91
  162.7 0.7 multiply_convert_fusion
  163.3 0.0 all-gather.7.cloned.1.call-update
  163.4 0.0 reduce-scatter.2.cloned.1.call-start
  163.4 63.0 %all-gather.7.cloned.1.call-done = bf16[64,8192]{0,1:T(8,128)(2,1)} async-done(((bf16[64,64]{0,1:T(8,128)(2,1)}), bf16[64,8192]{0,1:T(8,128)(2,1)}) %all-gather.7.cloned.1.call-update) | async-done | bytes 1048592 | tf_op jit(solution)/shard_map/all_gather | solution.py:94
  226.4 0.0 copy-start.1
  226.4 4.0 fusion.44
  230.5 0.0 copy-done.1
  230.5 9.4 %fusion.16 = f32[64,8192]{0,1:T(8,128)} fusion(bf16[224,8192]{1,0:T(8,128)(2,1)} %param.25, bf16[64,8192]{0,1:T(8,128)(2,1)S(1)} %copy-done.1, bf16[8192,224]{0,1:T(8,128)(2,1)} %param.24, f32[64,224]{1,0:T(8,128)S(1)} %fusion.44), kind=kOutput, calls=%fused_computation.18 | convolution fusion | flops 469848064 | bytes 10543104 | tf_op jit(solution)/shard_map/dot_general | solution.py:98
  239.8 0.0 reduce-scatter.2.cloned.1.call-update
  239.9 656.3 %reduce-scatter.2.cloned.1.call-done = f32[64,64]{0,1:T(8,128)} async-done(((f32[64,8192]{0,1:T(8,128)}), f32[64,64]{0,1:T(8,128)}) %reduce-scatter.2.cloned.1.call-update) | async-done | bytes 16400 | tf_op jit(solution)/shard_map/reduce_scatter | solution.py:99
  896.2 0.8 add_convert_fusion
  896.9 0.7 copy.22
  (16 shorter events, 0.1 us)
Async XLA Ops:
  6.5 91.5 %copy-start = (bf16[8192,64]{0,1:T(8,128)(2,1)S(1)}, bf16[8192,64]{0,1:T(8,128)(2,1)}, u32[]{:S(2)}) copy-start(bf16[8192,64]{0,1:T(8,128)(2,1)} %param.21) | copy-start | bytes 3145732
  6.5 90.1 %all-gather.9.cloned.1.call-start = ((), (), s32[]{:S(2)}) async-start(), calls=%async_computation.3 | async-start | bytes 1081344 | tf_op jit(solution)/shard_map/all_gather | solution.py:85
  6.5 24.3 %copy-start.2 = (bf16[2,1024,1024]{2,1,0:T(8,128)(2,1)S(1)}, bf16[2,1024,1024]{2,1,0:T(8,128)(2,1)}, u32[]{:S(2)}) copy-start(bf16[2,1024,1024]{2,1,0:T(8,128)(2,1)} %param.16) | copy-start | bytes 12582916
  11.2 30.3 %copy-start.5 = (bf16[2,1024]{1,0:T(2,128)(2,1)S(1)}, bf16[2,1024]{1,0:T(2,128)(2,1)}, u32[]{:S(2)}) copy-start(bf16[2,1024]{1,0:T(2,128)(2,1)} %param.17) | copy-start | bytes 12292
  11.2 30.3 %copy-start.3 = (bf16[2,8192]{1,0:T(2,128)(2,1)S(1)}, bf16[2,8192]{1,0:T(2,128)(2,1)}, u32[]{:S(2)}) copy-start(bf16[2,8192]{1,0:T(2,128)(2,1)} %param.14) | copy-start | bytes 98308
  11.2 30.4 %copy-start.6 = (bf16[2,1024]{1,0:T(2,128)(2,1)S(1)}, bf16[2,1024]{1,0:T(2,128)(2,1)}, u32[]{:S(2)}) copy-start(bf16[2,1024]{1,0:T(2,128)(2,1)} %param.18) | copy-start | bytes 12292
  30.8 12.2 %copy-start.7 = (bf16[64]{0:T(256)(128)(2,1)S(1)}, bf16[64]{0:T(256)(128)(2,1)}, u32[]{:S(2)}) copy-start(bf16[64]{0:T(256)(128)(2,1)} %param.22) | copy-start | bytes 388
  30.8 12.2 %copy-start.4 = (bf16[64,64]{1,0:T(8,128)(2,1)S(1)}, bf16[64,64]{1,0:T(8,128)(2,1)}, u32[]{:S(2)}) copy-start(bf16[64,64]{1,0:T(8,128)(2,1)} %param.20) | copy-start | bytes 24580
  42.9 183.5 %all-gather.7.cloned.1.call-start = ((), (), s32[]{:S(2)}) async-start(), calls=%async_computation.1 | async-start | bytes 2113536 | tf_op jit(solution)/shard_map/all_gather | solution.py:94
  163.4 732.8 %reduce-scatter.2.cloned.1.call-start = ((), (), s32[]{:S(2)}) async-start(), calls=%async_computation.2 | async-start | bytes 4227072 | tf_op jit(solution)/shard_map/reduce_scatter | solution.py:99
  226.4 4.0 copy-start.1
Sparse Core Ops, SparseCore 0:
  43.1 53.4 all-gather.8
  163.5 62.8 all-gather.6
  240.0 656.1 reduce-scatter.1
where the time goes:
time: 904 us
  waiting for transfers between devices  773 us (86%)
  blocking collectives  93.1 us (10%)
  matrix products  18.7 us (2%)
  between operations  13.3 us (1%)
    reduce_scatter x1, waiting for transfers between devices, on_device(): lax.psum_scatter(down_terms, ('side', 'wide', 'narrow'), scatter_dimensio...  656 us
    psum x1, blocking collectives, on_device(): lax.psum(jnp.sum(stream_f * stream_f, axis=-1), ('side', 'wide', 'narrow'))  64.1 us
    all_gather x1, waiting for transfers between devices, on_device(): lax.all_gather(normed, ('side', 'wide', 'narrow'), axis=1, tiled=True)  63 us
    all_gather x1, waiting for transfers between devices, on_device(): lax.all_gather(attended, ('side', 'wide'), axis=0, tiled=True)  53.5 us
    all_gather x3, blocking collectives, combined_all(): pieces = jax.tree.map(lambda part: lax.all_gather(part, axis), value)  29 us
  transfers between devices with their start and end apart: 3, of which 3 were waited for; matrix products, arithmetic and copies ran while one was open for 0% of the time, Pallas kernels for 0%

commit v1 on v0

v1 whole, which is shorter than its diff:
```python
import jax
import jax.numpy as jnp
from jax import lax
from jax.experimental import pallas as pl
from jax.experimental.pallas import tpu as pltpu
from jax.sharding import PartitionSpec as P

D = 8192
HEAD = 128
SPAN = 1024
UNITS = 224
SCALE = HEAD**-0.5
NEG = -1e30
MESH = pl.DeviceIdType.MESH
F32 = jnp.float32
BF16 = jnp.bfloat16
NT = (((1,), (1,)), ((), ()))


def dot_nt(a, b):
    return lax.dot_general(a, b, NT, preferred_element_type=F32)


def dot_nn(a, b):
    return jnp.dot(a, b, preferred_element_type=F32)


def layer_kernel(
    q_ref, lk_ref, lv_ref, len_ref, res_ref, gain_ref,
    k_hbm, v_hbm, o_hbm, g_hbm, u_hbm, d_hbm,
    out_ref,
    kv, vv, ow, gw, uw, dw,
    qrow, lrow, csend, crecv, ag1, wide1, ag2, rsend, rrecv,
    resin, gainin, stream, gains, fsend, frecv,
    kvsem, wsem, wssem, wrsem, smallsem, smallrs,
    cssem, crsem, gssem, grsem, as1, ar1, as2, ar2, rss, rsr, fs, fr,
    ready,
):
    s = lax.axis_index("side")
    w = lax.axis_index("wide")
    x = lax.axis_index("narrow")
    z, y = w // 4, w % 4
    me = w * 4 + x
    other = (1 - s, w, x)

    def at(zz, yy, xx):
        return (s, zz * 4 + yy, xx)

    lines = [at(z, y, (x + k) % 4) for k in (1, 2, 3)]
    lines += [at(z, (y + k) % 4, x) for k in (1, 2, 3)]
    lines += [at((z + k) % 4, y, x) for k in (1, 2, 3)]

    def remote(src, dst, ssem, rsem, dev):
        return pltpu.make_async_remote_copy(
            src_ref=src, dst_ref=dst, send_sem=ssem, recv_sem=rsem,
            device_id=dev, device_id_type=MESH,
        )

    loads = []
    for i in range(2):
        for src, dst, j in ((k_hbm, kv, 0), (v_hbm, vv, 1)):
            c = pltpu.make_async_copy(src.at[i], dst.at[i], kvsem.at[2 * i + j])
            c.start()
            loads.append(c)
    barrier = pltpu.get_barrier_semaphore()
    for dev in lines + [other]:
        pl.semaphore_signal(barrier, inc=1, device_id=dev, device_id_type=MESH)
    weights = []
    for i, (src, dst, n) in enumerate(
        ((o_hbm, ow, 64), (g_hbm, gw, UNITS), (u_hbm, uw, UNITS), (d_hbm, dw, UNITS))
    ):
        dst = dst.at[pl.ds(s * 64, 64)] if i == 0 else dst.at[s]
        c = pltpu.make_async_copy(src, dst, wsem.at[i])
        c.start()
        weights.append((c, src, dst))

    qf = q_ref[...].astype(F32)
    for h in range(64):
        qrow[pl.ds(h, 2, stride=64), :] = qf[:, h * HEAD : (h + 1) * HEAD]
    for j, ref in enumerate((lk_ref, lv_ref)):
        lf = ref[...].astype(F32)
        for g in range(8):
            lrow[pl.ds(16 * j + g, 2, stride=8), :] = lf[:, g * HEAD : (g + 1) * HEAD]

    lane = lax.broadcasted_iota(jnp.int32, (1, HEAD), 1)
    low = lane < 64
    positions = x * SPAN + lax.broadcasted_iota(jnp.int32, (1, SPAN), 1)
    zero8 = jnp.zeros((8, HEAD), F32)

    def attend(i):
        valid = positions < len_ref[i]
        loads[2 * i].wait()
        for p in range(4):
            q16 = qrow[pl.ds(64 * i + 16 * p, 16), :]
            qa, qb = q16[:8], q16[8:]
            pair = jnp.concatenate(
                [jnp.concatenate([qa, zero8], 1), jnp.concatenate([zero8, qb], 1)], 0
            ).astype(BF16)
            lanes = slice(256 * p, 256 * (p + 1))
            score = dot_nt(pair, kv[i, :, lanes]) * SCALE
            score = jnp.where(valid, score, NEG)
            top = jnp.max(score, axis=1, keepdims=True)
            weight = jnp.where(valid, jnp.exp(score - top), 0.0)
            den = jnp.sum(weight, axis=1, keepdims=True)
            if p == 0:
                loads[2 * i + 1].wait()
            both = dot_nn(weight.astype(BF16), vv[i, :, lanes])
            num = jnp.concatenate([both[:8, :HEAD], both[8:, HEAD:]], 0)
            def rows(j):
                a = lrow[pl.ds(16 * j + 8 * i + 2 * p, 1), :]
                b = lrow[pl.ds(16 * j + 8 * i + 2 * p + 1, 1), :]
                return jnp.concatenate(
                    [jnp.broadcast_to(a, (8, HEAD)), jnp.broadcast_to(b, (8, HEAD))], 0
                )
            fresh = jnp.sum(q16 * rows(0), axis=1, keepdims=True) * SCALE
            fresh = jnp.where(x == 0, fresh, NEG)
            peak = jnp.maximum(top, fresh)
            shrink = jnp.exp(top - peak)
            own = jnp.where(x == 0, jnp.exp(fresh - peak), 0.0)
            num = num * shrink + own * rows(1)
            den = den * shrink + own
            m1 = peak.astype(BF16).astype(F32)
            m2 = (peak - m1).astype(BF16).astype(F32)
            m3 = (peak - m1) - m2
            d1 = den.astype(BF16).astype(F32)
            d2 = den - d1
            coded = jnp.where(
                lane == 0, m1,
                jnp.where(lane == 1, m2, jnp.where(lane == 2, m3, jnp.where(lane == 3, d1, d2))),
            )
            csend[p, pl.ds(16 * i, 16), :] = num.astype(BF16)
            csend[p, pl.ds(32 + 16 * i, 16), :] = coded.astype(BF16)

    attend(0)
    attend(1)

    pl.semaphore_wait(barrier, 10)
    combine = []
    for j, k in enumerate((2, 1, 3)):
        xx = (x + k) % 4
        c = remote(csend.at[xx], crecv.at[x], cssem, crsem, at(z, y, xx))
        c.start()
        combine.append(c)
    for dev in lines:
        pl.semaphore_signal(ready.at[0], inc=1, device_id=dev, device_id_type=MESH)

    small = [
        remote(res_ref.at[pl.ds((1 - s) * 32, 32)], resin, smallsem.at[0], smallrs.at[0], other),
        remote(gain_ref, gainin, smallsem.at[1], smallrs.at[1], other),
    ]
    for c in small:
        c.start()
    sends = []
    for i, (c, src, dst) in enumerate(weights):
        c = remote(src, dst, wssem.at[i], wrsem.at[i], other)
        c.start()
        sends.append(c)

    def halves(own, theirs):
        first = jnp.where(s == 0, own, theirs)
        second = jnp.where(s == 0, theirs, own)
        return jnp.concatenate([first, second], axis=1)

    for c in small:
        c.wait_recv()
    stream[...] = halves(
        res_ref[pl.ds(s * 32, 32), :].astype(F32), resin[...].astype(F32)
    )
    gains[me] = halves(gain_ref[...], gainin[...])

    def gain_stage(j, start, count, devs):
        part = gains.at[pl.ds(start, count)]
        cs = []
        for dev in devs:
            c = remote(part, part, gssem.at[j], grsem.at[j], dev)
            c.start()
            cs.append(c)
        return cs

    def settle(sem, ref, send=False):
        c = remote(ref, ref, sem, sem, other)
        if send:
            c.wait_send()
        else:
            c.wait_recv()

    gain_stage(0, me, 1, lines[:3])
    pl.semaphore_wait(ready.at[0], 9)
    for dev in lines:
        pl.semaphore_signal(ready.at[1], inc=1, device_id=dev, device_id_type=MESH)

    settle(crsem, crecv.at[pl.ds(0, 3)])
    crecv[x] = csend[x]
    parts = []
    for i in range(4):
        code = crecv[i, 32:64, :].astype(F32)
        m = code[:, 0:1] + code[:, 1:2] + code[:, 2:3]
        d = code[:, 3:4] + code[:, 4:5]
        parts.append((m, d, crecv[i, 0:32, :].astype(F32)))
    peak = jnp.maximum(
        jnp.maximum(parts[0][0], parts[1][0]), jnp.maximum(parts[2][0], parts[3][0])
    )
    num, den = 0.0, 0.0
    for m, d, n in parts:
        f = jnp.exp(m - peak)
        num = num + n * f
        den = den + d * f
    ag1[me] = (num / den).astype(BF16)

    pl.semaphore_wait(ready.at[1], 9)

    order = (2, 1, 3, 0)

    def spread(buf, ssem, rsem, by):
        for g in order:
            def step(i, carry, g=g):
                a, b = i // 4, i % 4
                if by == "x":
                    dev = at((z + a) % 4, (y + b) % 4, (x + g) % 4)
                else:
                    dev = at((z + g) % 4, (y + a) % 4, (x + b) % 4)
                remote(buf.at[me], buf.at[me], ssem, rsem.at[g], dev).start()
                return carry
            lax.fori_loop(1 if g == 0 else 0, 16, step, 0)

    spread(ag1, as1, ar1, "x")

    settle(grsem.at[0], gains.at[pl.ds(0, 3)])
    gain_stage(1, w * 4, 4, lines[3:6])

    weights[0][0].wait()
    sends[0].wait_recv()
    total = stream[...]
    for g in order:
        settle(ar1.at[g], ag1.at[pl.ds(0, 15 if g == 0 else 16)])
        xx = (x + 4 - g) % 4
        for n in range(16):
            wide1[g, pl.ds(32 * n, 32), :] = ag1[4 * n + xx].astype(F32)
        rows = jnp.concatenate(
            [wide1[g, pl.ds(h, 32, stride=16), :].astype(BF16) for h in range(16)], axis=1
        )
        total = total + dot_nt(rows, ow[:, pl.ds(pl.multiple_of(xx * 2048, 2048), 2048)])
    rounded = total.astype(BF16)
    stream[...] = rounded.astype(F32)
    ag2[me] = rounded

    spread(ag2, as2, ar2, "z")

    settle(grsem.at[1], gains.at[pl.ds(0, 12)])
    gain_stage(2, z * 16, 16, lines[6:9])
    for c, _, _ in weights[1:3]:
        c.wait()
    for c in sends[1:3]:
        c.wait_recv()
    settle(grsem.at[2], gains.at[pl.ds(0, 48)])

    squares = jnp.zeros((32, HEAD), F32)
    gate = [jnp.zeros((32, UNITS), F32) for _ in range(2)]
    up = [jnp.zeros((32, UNITS), F32) for _ in range(2)]
    for g in order:
        settle(ar2.at[g], ag2.at[pl.ds(0, 15 if g == 0 else 16)])
        zz = (z + 4 - g) % 4
        firsts, seconds = [], []
        for t in range(8):
            c = zz * 16 + 2 * t
            a, b = ag2[c].astype(F32), ag2[c + 1].astype(F32)
            squares = squares + a * a + b * b
            a = a * gains[c][0:1]
            b = b * gains[c + 1][0:1]
            firsts.append(jnp.where(low, a, pltpu.roll(b, 64, 1)).astype(BF16))
            seconds.append(jnp.where(low, pltpu.roll(a, 64, 1), b).astype(BF16))
        first = jnp.concatenate(firsts, axis=1)
        second = jnp.concatenate(seconds, axis=1)
        at0 = pl.ds(pl.multiple_of(zz * 1024, 1024), 1024)
        at1 = pl.ds(pl.multiple_of(4096 + zz * 1024, 1024), 1024)
        for e in range(2):
            gate[e] = gate[e] + dot_nt(first, gw[e, :, at0]) + dot_nt(second, gw[e, :, at1])
            up[e] = up[e] + dot_nt(first, uw[e, :, at0]) + dot_nt(second, uw[e, :, at1])
    inverse = lax.rsqrt(jnp.sum(squares, axis=1, keepdims=True) / D + 1e-05)
    hidden = []
    for e in range(2):
        v = gate[e] * inverse
        hidden.append((v / (1.0 + jnp.exp(-v)) * (up[e] * inverse)).astype(BF16))

    weights[3][0].wait()
    sends[3].wait_recv()
    for g in order:
        zz = (z + g) % 4
        at0 = pl.ds(pl.multiple_of(zz * 1024, 1024), 1024)
        at1 = pl.ds(pl.multiple_of(4096 + zz * 1024, 1024), 1024)
        first = dot_nn(hidden[0], dw[0, :, at0]) + dot_nn(hidden[1], dw[1, :, at0])
        second = dot_nn(hidden[0], dw[0, :, at1]) + dot_nn(hidden[1], dw[1, :, at1])
        for t in range(8):
            a = first[:, HEAD * t : HEAD * (t + 1)]
            b = second[:, HEAD * t : HEAD * (t + 1)]
            rsend[zz * 16 + 2 * t] = jnp.where(low, a, pltpu.roll(b, 64, 1)).astype(BF16)
            rsend[zz * 16 + 2 * t + 1] = jnp.where(low, pltpu.roll(a, 64, 1), b).astype(BF16)

        def step(i, carry, zz=zz, g=g):
            yy, xx = (y + i // 4) % 4, (x + i % 4) % 4
            remote(
                rsend.at[zz * 16 + yy * 4 + xx], rrecv.at[me], rss, rsr.at[g], at(zz, yy, xx)
            ).start()
            return carry

        lax.fori_loop(1 if g == 0 else 0, 16, step, 0)
    rrecv[me] = rsend[me]

    total = stream[...]
    for g in order:
        settle(rsr.at[g], rrecv.at[pl.ds(0, 15 if g == 0 else 16)])
        zz = (z + 4 - g) % 4
        part = rrecv[zz * 16].astype(F32)
        for n in range(1, 16):
            part = part + rrecv[zz * 16 + n].astype(F32)
        total = total + part
    turned = pltpu.roll(total, 64, 1)
    mine = jnp.where(s == 0, total, turned)[:, :64].astype(BF16)
    theirs = jnp.where(s == 0, turned, total)[:, :64].astype(BF16)
    fsend[...] = theirs
    last = remote(fsend, frecv, fs, fr, other)
    last.start()
    out_ref[pl.ds(s * 32, 32), :] = mine

    settle(cssem, csend.at[pl.ds(0, 3)], True)
    for c in small + sends:
        c.wait_send()
    settle(gssem.at[0], gains.at[pl.ds(0, 3)], True)
    settle(gssem.at[1], gains.at[pl.ds(0, 12)], True)
    settle(gssem.at[2], gains.at[pl.ds(0, 48)], True)
    settle(as1, ag1.at[pl.ds(0, 63)], True)
    settle(as2, ag2.at[pl.ds(0, 63)], True)
    settle(rss, rsend.at[pl.ds(0, 63)], True)
    last.wait()
    out_ref[pl.ds((1 - s) * 32, 32), :] = frecv[...]


def on_device(
    queries, key_cache, value_cache, latest_key, latest_value, lengths,
    residual, o_weight, norm_gain, gate_weight, up_weight, down_weight,
):
    gain = jnp.broadcast_to(norm_gain.astype(F32)[None, :], (8, 64))
    vmem = pl.BlockSpec(memory_space=pltpu.VMEM)
    smem = pl.BlockSpec(memory_space=pltpu.SMEM)
    hbm = pl.BlockSpec(memory_space=pl.ANY)
    dma = pltpu.SemaphoreType.DMA
    return pl.pallas_call(
        layer_kernel,
        out_shape=jax.ShapeDtypeStruct((64, 64), BF16),
        in_specs=[vmem, vmem, vmem, smem, vmem, vmem] + [hbm] * 6,
        out_specs=vmem,
        scratch_shapes=[
            pltpu.VMEM((2, SPAN, 1024), BF16),
            pltpu.VMEM((2, SPAN, 1024), BF16),
            pltpu.VMEM((128, D), BF16),
            pltpu.VMEM((2, UNITS, D), BF16),
            pltpu.VMEM((2, UNITS, D), BF16),
            pltpu.VMEM((2, UNITS, D), BF16),
            pltpu.VMEM((128, HEAD), F32),
            pltpu.VMEM((32, HEAD), F32),
            pltpu.VMEM((4, 64, HEAD), BF16),
            pltpu.VMEM((4, 64, HEAD), BF16),
            pltpu.VMEM((64, 32, HEAD), BF16),
            pltpu.VMEM((4, 512, HEAD), F32),
            pltpu.VMEM((64, 32, HEAD), BF16),
            pltpu.VMEM((64, 32, HEAD), BF16),
            pltpu.VMEM((64, 32, HEAD), BF16),
            pltpu.VMEM((32, 64), BF16),
            pltpu.VMEM((8, 64), F32),
            pltpu.VMEM((32, HEAD), F32),
            pltpu.VMEM((64, 8, HEAD), F32),
            pltpu.VMEM((32, 64), BF16),
            pltpu.VMEM((32, 64), BF16),
            dma((4,)), dma((4,)), dma((4,)), dma((4,)), dma((2,)), dma((2,)),
            dma, dma, dma((3,)), dma((3,)),
            dma, dma((4,)), dma, dma((4,)), dma, dma((4,)), dma, dma,
            pltpu.SemaphoreType.REGULAR((2,)),
        ],
        compiler_params=pltpu.CompilerParams(
            collective_id=0, has_side_effects=True, vmem_limit_bytes=52 << 20
        ),
    )(
        queries, latest_key, latest_value, lengths, residual, gain,
        key_cache, value_cache, o_weight.T, gate_weight.T, up_weight.T, down_weight,
    )


def solution(mesh):
    sessions = ("side", "wide")
    every = ("side", "wide", "narrow")
    return jax.shard_map(
        on_device,
        mesh=mesh,
        in_specs=(
            P(sessions, None),
            P(sessions, "narrow", None),
            P(sessions, "narrow", None),
            P(sessions, None),
            P(sessions, None),
            P(sessions),
            P(None, every),
            P(None, every),
            P(every),
            P(None, every),
            P(None, every),
            P(every, None),
        ),
        out_specs=P(None, every),
        check_vma=False,
    )
```

time: 904 us -> 60.6 us (0.07)
  waiting for transfers between devices: 773 us -> 0 us
  blocking collectives: 93.1 us -> 0 us
  Pallas kernels: 0 us -> 54.3 us
  matrix products: 18.7 us -> 0 us
  between operations: 13.3 us -> 0.02 us
    reduce_scatter x1 -> x0, waiting for transfers between devices: 656 us -> none  [on_device(): lax.psum_scatter(down_terms, ('side', 'wide', 'narrow'), scatter_dimensio...]
    all_gather x2 -> x0, waiting for transfers between devices: 116 us -> none  [the longest x1 63 us: on_device(): lax.all_gather(normed, ('side', 'wide', 'narrow'), axis=1, tiled=True)]
    psum x1 -> x0, blocking collectives: 64.1 us -> none  [on_device(): lax.psum(jnp.sum(stream_f * stream_f, axis=-1), ('side', 'wide', 'narrow'))]
    pallas_call x0 -> x1, Pallas kernels: none -> 54.3 us  [on_device(): pl.pallas_call(layer_kernel, out_shape=jax.ShapeDtypeStruct((64, 64), BF1...]
    all_gather x3 -> x0, blocking collectives: 29 us -> none  [combined_all(): pieces = jax.tree.map(lambda part: lax.all_gather(part, axis), value)]
    dot_general x6 -> x0, matrix products: 18.7 us -> none  [the longest x1 9.38 us: on_device(): jnp.dot(hidden, down_weight, preferred_element_type=jnp.float32)]
  transfers between devices with their start and end apart: 3 -> 0, of which waited for: 3 -> 0; matrix products, arithmetic and copies ran while one was open for 0% -> 0% of each run, Pallas kernels for 0% -> 0%
where the time goes in v1:
time: 60.6 us; the launch traced here: 60.3 us
  Pallas kernels  54.3 us (90%)
  local copies, waits for them, and re-layouts  5.99 us (10%)
    pallas_call x1, Pallas kernels, on_device(): pl.pallas_call(layer_kernel, out_shape=jax.ShapeDtypeStruct((64, 64), BF1...  54.3 us
    unnamed x13, local copies, waits for them, and re-layouts  5.33 us

profile of v1, /device:TPU:1, one launch (start us, length us, event | category | flops | bytes accessed | tf_op | source)
XLA Modules:
  0.0 60.3 jit_solution(17664917702810369312)
XLA Ops:
  0.0 0.7 %broadcast_in_dim.2.gain_ref = f32[8,64]{1,0:T(8,128)S(1)} broadcast(bf16[64]{0:T(256)(128)(2,1)} %param.20), dimensions={1} | broadcast | bytes 2176 | tf_op jit(solution)/shard_map/broadcast_in_dim | solution.py:342
  0.7 0.0 copy-start
  0.7 1.2 %copy-done = bf16[8192,64]{0,1:T(8,128)(2,1)S(1)} copy-done((bf16[8192,64]{0,1:T(8,128)(2,1)S(1)}, bf16[8192,64]{0,1:T(8,128)(2,1)}, u32[]{:S(2)}) %copy-start) | copy-done | bytes 1048600
  1.9 0.0 copy-start.1
  1.9 0.8 %copy-done.1 = bf16[2,8192]{1,0:T(2,128)(2,1)S(1)} copy-done((bf16[2,8192]{1,0:T(2,128)(2,1)S(1)}, bf16[2,8192]{1,0:T(2,128)(2,1)}, u32[]{:S(2)}) %copy-start.1) | copy-done | bytes 32792
  2.6 0.0 copy-start.2
  2.6 0.7 %copy-done.2 = bf16[64,64]{1,0:T(8,128)(2,1)S(1)} copy-done((bf16[64,64]{1,0:T(8,128)(2,1)S(1)}, bf16[64,64]{1,0:T(8,128)(2,1)}, u32[]{:S(2)}) %copy-start.2) | copy-done | bytes 8216
  3.4 0.0 copy-start.3
  3.4 0.7 %copy-done.3 = bf16[2,1024]{1,0:T(2,128)(2,1)S(1)} copy-done((bf16[2,1024]{1,0:T(2,128)(2,1)S(1)}, bf16[2,1024]{1,0:T(2,128)(2,1)}, u32[]{:S(2)}) %copy-start.3) | copy-done | bytes 4120
  4.0 0.0 copy-start.4
  4.0 0.7 %copy-done.4 = bf16[2,1024]{1,0:T(2,128)(2,1)S(1)} copy-done((bf16[2,1024]{1,0:T(2,128)(2,1)S(1)}, bf16[2,1024]{1,0:T(2,128)(2,1)}, u32[]{:S(2)}) %copy-start.4) | copy-done | bytes 4120
  4.7 0.0 copy-start.5
  4.7 0.7 %copy-done.5 = s32[2]{0:T(128)S(1)} copy-done((s32[2]{0:T(128)S(1)}, s32[2]{0:T(128)}, u32[]{:S(2)}) %copy-start.5) | copy-done | bytes 32
  5.4 54.3 %shard_map.118 = bf16[64,64]{1,0:T(8,128)(2,1)S(1)} custom-call(bf16[2,8192]{1,0:T(2,128)(2,1)S(1)} %copy-done.1, bf16[2,1024]{1,0:T(2,128)(2,1)S(1)} %copy-done.3, bf16[2,1024]{1,0:T(2,128)(2,1)S(1)} %copy-done.4, s32[2]{0:T(128)S(1)} %copy-done.5, bf16[64,64]{1,0:T(8,128)(2,1)S(1)} %copy-done.2, f32[8,64]{1,0:T(8,128)S(1)} %broadcast_in_dim.2.gain_ref, ...), custom_call_target="tpu_custom_call" | custom-call | tf_op jit(solution)/shard_map/pallas_call | solution.py:347
  59.7 0.6 %copy.14 = bf16[64,64]{1,0:T(8,128)(2,1)} copy(bf16[64,64]{1,0:T(8,128)(2,1)S(1)} %shard_map.118) | data formatting | bytes 16384
Async XLA Ops:
  0.7 1.2 %copy-start = (bf16[8192,64]{0,1:T(8,128)(2,1)S(1)}, bf16[8192,64]{0,1:T(8,128)(2,1)}, u32[]{:S(2)}) copy-start(bf16[8192,64]{0,1:T(8,128)(2,1)} %param.19) | copy-start | bytes 3145732
  1.9 0.8 %copy-start.1 = (bf16[2,8192]{1,0:T(2,128)(2,1)S(1)}, bf16[2,8192]{1,0:T(2,128)(2,1)}, u32[]{:S(2)}) copy-start(bf16[2,8192]{1,0:T(2,128)(2,1)} %q_ref.1) | copy-start | bytes 98308
  2.6 0.7 %copy-start.2 = (bf16[64,64]{1,0:T(8,128)(2,1)S(1)}, bf16[64,64]{1,0:T(8,128)(2,1)}, u32[]{:S(2)}) copy-start(bf16[64,64]{1,0:T(8,128)(2,1)} %res_ref.1) | copy-start | bytes 24580
  3.4 0.7 %copy-start.3 = (bf16[2,1024]{1,0:T(2,128)(2,1)S(1)}, bf16[2,1024]{1,0:T(2,128)(2,1)}, u32[]{:S(2)}) copy-start(bf16[2,1024]{1,0:T(2,128)(2,1)} %lk_ref.1) | copy-start | bytes 12292
  4.0 0.7 %copy-start.4 = (bf16[2,1024]{1,0:T(2,128)(2,1)S(1)}, bf16[2,1024]{1,0:T(2,128)(2,1)}, u32[]{:S(2)}) copy-start(bf16[2,1024]{1,0:T(2,128)(2,1)} %lv_ref.1) | copy-start | bytes 12292
  4.7 0.7 %copy-start.5 = (s32[2]{0:T(128)S(1)}, s32[2]{0:T(128)}, u32[]{:S(2)}) copy-start(s32[2]{0:T(128)} %len_ref.1) | copy-start | bytes 28

commit v2 on v1

--- a/solution.py
+++ b/solution.py
@@ -26,11 +26,12 @@
 
 
 def layer_kernel(
-    q_ref, lk_ref, lv_ref, len_ref, res_ref, gain_ref,
+    q_hbm, lk_hbm, lv_hbm, len_hbm, res_hbm, gain_hbm,
     k_hbm, v_hbm, o_hbm, g_hbm, u_hbm, d_hbm,
     out_ref,
+    q_ref, lk_ref, lv_ref, len_ref, res_ref, gain1, gain_ref, insem,
     kv, vv, ow, gw, uw, dw,
-    qrow, lrow, csend, crecv, ag1, wide1, ag2, rsend, rrecv,
+    qrow, lrow, csend, crecv, ag1, perm, ag2, gnat, rsend, rrecv,
     resin, gainin, stream, gains, fsend, frecv,
     kvsem, wsem, wssem, wrsem, smallsem, smallrs,
     cssem, crsem, gssem, grsem, as1, ar1, as2, ar2, rss, rsr, fs, fr,
@@ -56,6 +57,16 @@
             device_id=dev, device_id_type=MESH,
         )
 
+    inputs = []
+    for i, (src, dst) in enumerate(
+        (
+            (q_hbm, q_ref), (lk_hbm, lk_ref), (lv_hbm, lv_ref),
+            (len_hbm, len_ref), (res_hbm, res_ref), (gain_hbm, gain1),
+        )
+    ):
+        c = pltpu.make_async_copy(src, dst, insem.at[i])
+        c.start()
+        inputs.append(c)
     loads = []
     for i in range(2):
         for src, dst, j in ((k_hbm, kv, 0), (v_hbm, vv, 1)):
@@ -65,14 +76,9 @@
     barrier = pltpu.get_barrier_semaphore()
     for dev in lines + [other]:
         pl.semaphore_signal(barrier, inc=1, device_id=dev, device_id_type=MESH)
-    weights = []
-    for i, (src, dst, n) in enumerate(
-        ((o_hbm, ow, 64), (g_hbm, gw, UNITS), (u_hbm, uw, UNITS), (d_hbm, dw, UNITS))
-    ):
-        dst = dst.at[pl.ds(s * 64, 64)] if i == 0 else dst.at[s]
-        c = pltpu.make_async_copy(src, dst, wsem.at[i])
-        c.start()
-        weights.append((c, src, dst))
+    for c in inputs:
+        c.wait()
+    gain_ref[...] = jnp.broadcast_to(gain1[...].astype(F32)[None, :], (8, 64))
 
     qf = q_ref[...].astype(F32)
     for h in range(64):
@@ -87,52 +93,85 @@
     positions = x * SPAN + lax.broadcasted_iota(jnp.int32, (1, SPAN), 1)
     zero8 = jnp.zeros((8, HEAD), F32)
 
+    weights = []
+
+    def fetch():
+        for i, (src, dst, n) in enumerate(
+            ((o_hbm, ow, 64), (g_hbm, gw, UNITS), (u_hbm, uw, UNITS), (d_hbm, dw, UNITS))
+        ):
+            dst = dst.at[pl.ds(s * n, n)]
+            c = pltpu.make_async_copy(src, dst, wsem.at[i])
+            c.start()
+            weights.append((c, src, dst))
+
     def attend(i):
         valid = positions < len_ref[i]
+        queries = [qrow[pl.ds(64 * i + 16 * p, 16), :] for p in range(4)]
+        pairs = []
+        for q16 in queries:
+            pairs.append(
+                jnp.concatenate(
+                    [
+                        jnp.concatenate([q16[:8], zero8], 1),
+                        jnp.concatenate([zero8, q16[8:]], 1),
+                    ],
+                    0,
+                ).astype(BF16)
+            )
+
+        def repeated(j):
+            return jnp.concatenate(
+                [
+                    jnp.broadcast_to(lrow[pl.ds(16 * j + 8 * i + g, 1), :], (8, HEAD))
+                    for g in range(8)
+                ],
+                0,
+            )
+
+        fresh = jnp.sum(jnp.concatenate(queries, 0) * repeated(0), axis=1, keepdims=True) * SCALE
+        fresh = jnp.where(x == 0, fresh, NEG)
         loads[2 * i].wait()
+        score = jnp.concatenate(
+            [dot_nt(pairs[p], kv[i, :, 256 * p : 256 * (p + 1)]) for p in range(4)], 0
+        )
+        score = jnp.where(valid, score * SCALE, NEG)
+        top = jnp.max(score, axis=1, keepdims=True)
+        weight = jnp.where(valid, jnp.exp(score - top), 0.0)
+        den = jnp.sum(weight, axis=1, keepdims=True)
+        rounded = weight.astype(BF16)
+        loads[2 * i + 1].wait()
+        nums = []
         for p in range(4):
-            q16 = qrow[pl.ds(64 * i + 16 * p, 16), :]
-            qa, qb = q16[:8], q16[8:]
-            pair = jnp.concatenate(
-                [jnp.concatenate([qa, zero8], 1), jnp.concatenate([zero8, qb], 1)], 0
-            ).astype(BF16)
-            lanes = slice(256 * p, 256 * (p + 1))
-            score = dot_nt(pair, kv[i, :, lanes]) * SCALE
-            score = jnp.where(valid, score, NEG)
-            top = jnp.max(score, axis=1, keepdims=True)
-            weight = jnp.where(valid, jnp.exp(score - top), 0.0)
-            den = jnp.sum(weight, axis=1, keepdims=True)
-            if p == 0:
-                loads[2 * i + 1].wait()
-            both = dot_nn(weight.astype(BF16), vv[i, :, lanes])
-            num = jnp.concatenate([both[:8, :HEAD], both[8:, HEAD:]], 0)
-            def rows(j):
-                a = lrow[pl.ds(16 * j + 8 * i + 2 * p, 1), :]
-                b = lrow[pl.ds(16 * j + 8 * i + 2 * p + 1, 1), :]
-                return jnp.concatenate(
-                    [jnp.broadcast_to(a, (8, HEAD)), jnp.broadcast_to(b, (8, HEAD))], 0
-                )
-            fresh = jnp.sum(q16 * rows(0), axis=1, keepdims=True) * SCALE
-            fresh = jnp.where(x == 0, fresh, NEG)
-            peak = jnp.maximum(top, fresh)
-            shrink = jnp.exp(top - peak)
-            own = jnp.where(x == 0, jnp.exp(fresh - peak), 0.0)
-            num = num * shrink + own * rows(1)
-            den = den * shrink + own
-            m1 = peak.astype(BF16).astype(F32)
-            m2 = (peak - m1).astype(BF16).astype(F32)
-            m3 = (peak - m1) - m2
-            d1 = den.astype(BF16).astype(F32)
-            d2 = den - d1
-            coded = jnp.where(
-                lane == 0, m1,
-                jnp.where(lane == 1, m2, jnp.where(lane == 2, m3, jnp.where(lane == 3, d1, d2))),
-            )
-            csend[p, pl.ds(16 * i, 16), :] = num.astype(BF16)
-            csend[p, pl.ds(32 + 16 * i, 16), :] = coded.astype(BF16)
+            both = dot_nn(rounded[16 * p : 16 * p + 16], vv[i, :, 256 * p : 256 * (p + 1)])
+            nums += [both[:8, :HEAD], both[8:, HEAD:]]
+        num = jnp.concatenate(nums, 0)
+        peak = jnp.maximum(top, fresh)
+        shrink = jnp.exp(top - peak)
+        own = jnp.where(x == 0, jnp.exp(fresh - peak), 0.0)
+        num = num * shrink + own * repeated(1)
+        den = den * shrink + own
+        m1 = peak.astype(BF16).astype(F32)
+        m2 = (peak - m1).astype(BF16).astype(F32)
+        m3 = (peak - m1) - m2
+        d1 = den.astype(BF16).astype(F32)
+        d2 = den - d1
+        coded = jnp.where(
+            lane == 0, m1,
+            jnp.where(lane == 1, m2, jnp.where(lane == 2, m3, jnp.where(lane == 3, d1, d2))),
+        )
+        num, coded = num.astype(BF16), coded.astype(BF16)
+        for p in range(4):
+            csend[p, pl.ds(16 * i, 16), :] = num[16 * p : 16 * p + 16]
+            csend[p, pl.ds(32 + 16 * i, 16), :] = coded[16 * p : 16 * p + 16]
 
     attend(0)
+    fetch()
     attend(1)
+
+    r = lax.broadcasted_iota(jnp.int32, (256, 256), 0)
+    k = lax.broadcasted_iota(jnp.int32, (256, 256), 1)
+    source = (r % 16 // 2) * 32 + (r % 2) * 16 + r // 16
+    perm[...] = jnp.where(source == k, 1.0, 0.0).astype(BF16)
 
     pl.semaphore_wait(barrier, 10)
     combine = []
@@ -210,18 +249,26 @@
     pl.semaphore_wait(ready.at[1], 9)
 
     order = (2, 1, 3, 0)
+    arrival = (0, 1, 3, 2)
+
+    def each(g, step):
+        if g == 0:
+            lax.fori_loop(0, 10, step, 0)
+            lax.fori_loop(11, 16, step, 0)
+        else:
+            lax.fori_loop(0, 16, step, 0)
 
     def spread(buf, ssem, rsem, by):
         for g in order:
             def step(i, carry, g=g):
-                a, b = i // 4, i % 4
+                a, b = (i // 4 + 2) % 4, (i + 2) % 4
                 if by == "x":
                     dev = at((z + a) % 4, (y + b) % 4, (x + g) % 4)
                 else:
                     dev = at((z + g) % 4, (y + a) % 4, (x + b) % 4)
                 remote(buf.at[me], buf.at[me], ssem, rsem.at[g], dev).start()
                 return carry
-            lax.fori_loop(1 if g == 0 else 0, 16, step, 0)
+            each(g, step)
 
     spread(ag1, as1, ar1, "x")
 
@@ -231,56 +278,72 @@
     weights[0][0].wait()
     sends[0].wait_recv()
     total = stream[...]
-    for g in order:
+    for n, g in enumerate(arrival):
         settle(ar1.at[g], ag1.at[pl.ds(0, 15 if g == 0 else 16)])
         xx = (x + 4 - g) % 4
-        for n in range(16):
-            wide1[g, pl.ds(32 * n, 32), :] = ag1[4 * n + xx].astype(F32)
+        turned = []
+        for half in range(2):
+            rows = jnp.concatenate([ag1[4 * (8 * half + j) + xx] for j in range(8)], 0)
+            turned.append(dot_nn(perm[...], rows).astype(BF16))
         rows = jnp.concatenate(
-            [wide1[g, pl.ds(h, 32, stride=16), :].astype(BF16) for h in range(16)], axis=1
+            [
+                jnp.concatenate([part[16 * h : 16 * h + 16] for part in turned], 0)
+                for h in range(16)
+            ],
+            axis=1,
         )
         total = total + dot_nt(rows, ow[:, pl.ds(pl.multiple_of(xx * 2048, 2048), 2048)])
+        if n == 1:
+            settle(grsem.at[1], gains.at[pl.ds(0, 12)])
+            gain_stage(2, z * 16, 16, lines[6:9])
     rounded = total.astype(BF16)
     stream[...] = rounded.astype(F32)
     ag2[me] = rounded
 
     spread(ag2, as2, ar2, "z")
 
-    settle(grsem.at[1], gains.at[pl.ds(0, 12)])
-    gain_stage(2, z * 16, 16, lines[6:9])
+    def mixed(a, b):
+        m = pltpu.roll(jnp.where(low, b, a), 64, 1)
+        return jnp.where(low, a, m), jnp.where(low, m, b)
+
+    settle(grsem.at[2], gains.at[pl.ds(0, 48)])
+    for t in range(32):
+        first, second = mixed(gains[2 * t], gains[2 * t + 1])
+        gnat[:, HEAD * t : HEAD * (t + 1)] = jnp.concatenate([first, first], 0).astype(BF16)
+        gnat[:, 4096 + HEAD * t : 4096 + HEAD * (t + 1)] = jnp.concatenate(
+            [second, second], 0
+        ).astype(BF16)
     for c, _, _ in weights[1:3]:
         c.wait()
     for c in sends[1:3]:
         c.wait_recv()
-    settle(grsem.at[2], gains.at[pl.ds(0, 48)])
-
-    squares = jnp.zeros((32, HEAD), F32)
-    gate = [jnp.zeros((32, UNITS), F32) for _ in range(2)]
-    up = [jnp.zeros((32, UNITS), F32) for _ in range(2)]
-    for g in order:
+
+    squares = jnp.zeros((32, 32), F32)
+    gate = jnp.zeros((32, 2 * UNITS), F32)
+    up = jnp.zeros((32, 2 * UNITS), F32)
+    for g in arrival:
         settle(ar2.at[g], ag2.at[pl.ds(0, 15 if g == 0 else 16)])
         zz = (z + 4 - g) % 4
-        firsts, seconds = [], []
+        sides = [[], []]
         for t in range(8):
             c = zz * 16 + 2 * t
-            a, b = ag2[c].astype(F32), ag2[c + 1].astype(F32)
-            squares = squares + a * a + b * b
-            a = a * gains[c][0:1]
-            b = b * gains[c + 1][0:1]
-            firsts.append(jnp.where(low, a, pltpu.roll(b, 64, 1)).astype(BF16))
-            seconds.append(jnp.where(low, pltpu.roll(a, 64, 1), b).astype(BF16))
-        first = jnp.concatenate(firsts, axis=1)
-        second = jnp.concatenate(seconds, axis=1)
-        at0 = pl.ds(pl.multiple_of(zz * 1024, 1024), 1024)
-        at1 = pl.ds(pl.multiple_of(4096 + zz * 1024, 1024), 1024)
+            for e, part in enumerate(mixed(ag2[c].astype(F32), ag2[c + 1].astype(F32))):
+                sides[e].append(part.astype(BF16))
         for e in range(2):
-            gate[e] = gate[e] + dot_nt(first, gw[e, :, at0]) + dot_nt(second, gw[e, :, at1])
-            up[e] = up[e] + dot_nt(first, uw[e, :, at0]) + dot_nt(second, uw[e, :, at1])
-    inverse = lax.rsqrt(jnp.sum(squares, axis=1, keepdims=True) / D + 1e-05)
-    hidden = []
-    for e in range(2):
-        v = gate[e] * inverse
-        hidden.append((v / (1.0 + jnp.exp(-v)) * (up[e] * inverse)).astype(BF16))
+            part = jnp.concatenate(sides[e], axis=1)
+            squares = squares + dot_nt(part, part)
+            lanes = pl.ds(pl.multiple_of(4096 * e + zz * 1024, 1024), 1024)
+            row = gnat[:, lanes]
+            part = part * jnp.concatenate([row, row], 0)
+            gate = gate + dot_nt(part, gw[:, lanes])
+            up = up + dot_nt(part, uw[:, lanes])
+    diagonal = lax.broadcasted_iota(jnp.int32, (32, 32), 0) == lax.broadcasted_iota(
+        jnp.int32, (32, 32), 1
+    )
+    squares = jnp.sum(jnp.where(diagonal, squares, 0.0), axis=1, keepdims=True)
+    inverse = lax.rsqrt(squares / D + 1e-05)
+    v = gate * inverse
+    hidden = (v / (1.0 + jnp.exp(-v)) * (up * inverse)).astype(BF16)
 
     weights[3][0].wait()
     sends[3].wait_recv()
@@ -288,26 +351,26 @@
         zz = (z + g) % 4
         at0 = pl.ds(pl.multiple_of(zz * 1024, 1024), 1024)
         at1 = pl.ds(pl.multiple_of(4096 + zz * 1024, 1024), 1024)
-        first = dot_nn(hidden[0], dw[0, :, at0]) + dot_nn(hidden[1], dw[1, :, at0])
-        second = dot_nn(hidden[0], dw[0, :, at1]) + dot_nn(hidden[1], dw[1, :, at1])
+        first = dot_nn(hidden, dw[:, at0])
+        second = dot_nn(hidden, dw[:, at1])
         for t in range(8):
-            a = first[:, HEAD * t : HEAD * (t + 1)]
-            b = second[:, HEAD * t : HEAD * (t + 1)]
-            rsend[zz * 16 + 2 * t] = jnp.where(low, a, pltpu.roll(b, 64, 1)).astype(BF16)
-            rsend[zz * 16 + 2 * t + 1] = jnp.where(low, pltpu.roll(a, 64, 1), b).astype(BF16)
+            lanes = slice(HEAD * t, HEAD * (t + 1))
+            a, b = mixed(first[:, lanes], second[:, lanes])
+            rsend[zz * 16 + 2 * t] = a.astype(BF16)
+            rsend[zz * 16 + 2 * t + 1] = b.astype(BF16)
 
         def step(i, carry, zz=zz, g=g):
-            yy, xx = (y + i // 4) % 4, (x + i % 4) % 4
+            yy, xx = (y + i // 4 + 2) % 4, (x + i + 2) % 4
             remote(
                 rsend.at[zz * 16 + yy * 4 + xx], rrecv.at[me], rss, rsr.at[g], at(zz, yy, xx)
             ).start()
             return carry
 
-        lax.fori_loop(1 if g == 0 else 0, 16, step, 0)
+        each(g, step)
     rrecv[me] = rsend[me]
 
     total = stream[...]
-    for g in order:
+    for g in arrival:
         settle(rsr.at[g], rrecv.at[pl.ds(0, 15 if g == 0 else 16)])
         zz = (z + 4 - g) % 4
         part = rrecv[zz * 16].astype(F32)
@@ -339,30 +402,37 @@
     queries, key_cache, value_cache, latest_key, latest_value, lengths,
     residual, o_weight, norm_gain, gate_weight, up_weight, down_weight,
 ):
-    gain = jnp.broadcast_to(norm_gain.astype(F32)[None, :], (8, 64))
     vmem = pl.BlockSpec(memory_space=pltpu.VMEM)
-    smem = pl.BlockSpec(memory_space=pltpu.SMEM)
-    hbm = pl.BlockSpec(memory_space=pl.ANY)
+    hbm = pl.BlockSpec(memory_space=pltpu.HBM)
     dma = pltpu.SemaphoreType.DMA
     return pl.pallas_call(
         layer_kernel,
         out_shape=jax.ShapeDtypeStruct((64, 64), BF16),
-        in_specs=[vmem, vmem, vmem, smem, vmem, vmem] + [hbm] * 6,
+        in_specs=[hbm] * 12,
         out_specs=vmem,
         scratch_shapes=[
+            pltpu.VMEM((2, D), BF16),
+            pltpu.VMEM((2, 1024), BF16),
+            pltpu.VMEM((2, 1024), BF16),
+            pltpu.SMEM((2,), jnp.int32),
+            pltpu.VMEM((64, 64), BF16),
+            pltpu.VMEM((64,), BF16),
+            pltpu.VMEM((8, 64), F32),
+            dma((6,)),
             pltpu.VMEM((2, SPAN, 1024), BF16),
             pltpu.VMEM((2, SPAN, 1024), BF16),
             pltpu.VMEM((128, D), BF16),
-            pltpu.VMEM((2, UNITS, D), BF16),
-            pltpu.VMEM((2, UNITS, D), BF16),
-            pltpu.VMEM((2, UNITS, D), BF16),
+            pltpu.VMEM((2 * UNITS, D), BF16),
+            pltpu.VMEM((2 * UNITS, D), BF16),
+            pltpu.VMEM((2 * UNITS, D), BF16),
             pltpu.VMEM((128, HEAD), F32),
             pltpu.VMEM((32, HEAD), F32),
             pltpu.VMEM((4, 64, HEAD), BF16),
             pltpu.VMEM((4, 64, HEAD), BF16),
             pltpu.VMEM((64, 32, HEAD), BF16),
-            pltpu.VMEM((4, 512, HEAD), F32),
+            pltpu.VMEM((256, 256), BF16),
             pltpu.VMEM((64, 32, HEAD), BF16),
+            pltpu.VMEM((16, D), BF16),
             pltpu.VMEM((64, 32, HEAD), BF16),
             pltpu.VMEM((64, 32, HEAD), BF16),
             pltpu.VMEM((32, 64), BF16),
@@ -377,10 +447,10 @@
             pltpu.SemaphoreType.REGULAR((2,)),
         ],
         compiler_params=pltpu.CompilerParams(
-            collective_id=0, has_side_effects=True, vmem_limit_bytes=52 << 20
+            collective_id=0, has_side_effects=True, vmem_limit_bytes=64 << 20
         ),
     )(
-        queries, latest_key, latest_value, lengths, residual, gain,
+        queries, latest_key, latest_value, lengths, residual, norm_gain,
         key_cache, value_cache, o_weight.T, gate_weight.T, up_weight.T, down_weight,
     )
 

time: 60.6 us -> 51.9 us (0.86)
  local copies, waits for them, and re-layouts: 5.99 us -> 1.32 us
  Pallas kernels: 54.3 us -> 50.4 us
    unnamed x13 -> x1, local copies, waits for them, and re-layouts: 5.33 us -> 1.32 us
    pallas_call x1, Pallas kernels: 54.3 us -> 50.4 us  [on_device(): pl.pallas_call(layer_kernel, out_shape=jax.ShapeDtypeStruct((64, 64), BF1...]
    broadcast_in_dim x1 -> x0, local copies, waits for them, and re-layouts: 0.66 us -> none  [on_device(): gain = jnp.broadcast_to(norm_gain.astype(F32)[None, :], (8, 64))]
where the time goes in v2:
time: 51.9 us; the launch traced here: 51.7 us
  Pallas kernels  50.4 us (97%)
  local copies, waits for them, and re-layouts  1.32 us (3%)
    pallas_call x1, Pallas kernels, on_device(): pl.pallas_call(layer_kernel, out_shape=jax.ShapeDtypeStruct((64, 64), BF1...  50.4 us
    unnamed x1, local copies, waits for them, and re-layouts  1.32 us

profile of v2, /device:TPU:1, one launch (start us, length us, event | category | flops | bytes accessed | tf_op | source)
XLA Modules:
  0.0 51.7 jit_solution(15725750526988834459)
XLA Ops:
  0.0 50.4 %shard_map.118 = bf16[64,64]{1,0:T(8,128)(2,1)} custom-call(bf16[2,8192]{1,0:T(2,128)(2,1)} %q_hbm.1, bf16[2,1024]{1,0:T(2,128)(2,1)} %lk_hbm.1, bf16[2,1024]{1,0:T(2,128)(2,1)} %lv_hbm.1, s32[2]{0:T(128)} %len_hbm.1, bf16[64,64]{1,0:T(8,128)(2,1)} %res_hbm.1, bf16[64]{0:T(256)(128)(2,1)} %gain_hbm.1, bf16[2,1024,1024]{2,1,0:T(8,128)(2,1)} %k_hbm.1, ...), custom_call_target="tpu_custom_call" | custom-call | tf_op jit(solution)/shard_map/pallas_call | solution.py:408
  50.4 1.3 %copy.14 = bf16[64,64]{1,0:T(8,128)(2,1)} copy(bf16[64,64]{1,0:T(8,128)(2,1)} %shard_map.118) | data formatting | bytes 16384

commit v3 on v2

--- a/solution.py
+++ b/solution.py
@@ -248,7 +248,7 @@
 
     pl.semaphore_wait(ready.at[1], 9)
 
-    order = (2, 1, 3, 0)
+    order = (0, 2, 1, 3)
     arrival = (0, 1, 3, 2)
 
     def each(g, step):
@@ -297,7 +297,6 @@
             settle(grsem.at[1], gains.at[pl.ds(0, 12)])
             gain_stage(2, z * 16, 16, lines[6:9])
     rounded = total.astype(BF16)
-    stream[...] = rounded.astype(F32)
     ag2[me] = rounded
 
     spread(ag2, as2, ar2, "z")
@@ -305,6 +304,14 @@
     def mixed(a, b):
         m = pltpu.roll(jnp.where(low, b, a), 64, 1)
         return jnp.where(low, a, m), jnp.where(low, m, b)
+
+    kept = rounded.astype(F32)
+    turned = pltpu.roll(kept, 64, 1)
+    kept, turned = kept[:, :64], turned[:, :64]
+    fsend[...] = jnp.where(s == 0, turned, kept).astype(BF16)
+    mine = jnp.where(s == 0, kept, turned)
+    swap = remote(fsend, frecv, fs, fr, other)
+    swap.start()
 
     settle(grsem.at[2], gains.at[pl.ds(0, 48)])
     for t in range(32):
@@ -347,7 +354,7 @@
 
     weights[3][0].wait()
     sends[3].wait_recv()
-    for g in order:
+    for g in (2, 1, 3, 0):
         zz = (z + g) % 4
         at0 = pl.ds(pl.multiple_of(zz * 1024, 1024), 1024)
         at1 = pl.ds(pl.multiple_of(4096 + zz * 1024, 1024), 1024)
@@ -355,35 +362,39 @@
         second = dot_nn(hidden, dw[:, at1])
         for t in range(8):
             lanes = slice(HEAD * t, HEAD * (t + 1))
-            a, b = mixed(first[:, lanes], second[:, lanes])
-            rsend[zz * 16 + 2 * t] = a.astype(BF16)
-            rsend[zz * 16 + 2 * t + 1] = b.astype(BF16)
+            for e, part in enumerate((first[:, lanes], second[:, lanes])):
+                a, b = mixed(part[:16], part[16:])
+                rsend[zz * 16 + 2 * t, e] = a.astype(BF16)
+                rsend[zz * 16 + 2 * t + 1, e] = b.astype(BF16)
 
         def step(i, carry, zz=zz, g=g):
             yy, xx = (y + i // 4 + 2) % 4, (x + i + 2) % 4
-            remote(
-                rsend.at[zz * 16 + yy * 4 + xx], rrecv.at[me], rss, rsr.at[g], at(zz, yy, xx)
-            ).start()
+            c = zz * 4 + yy
+            for e in range(2):
+                remote(
+                    rsend.at[c * 4 + xx, e], rrecv.at[s, me], rss, rsr.at[g], (e, c, xx)
+                ).start()
             return carry
 
         each(g, step)
-    rrecv[me] = rsend[me]
-
-    total = stream[...]
+    remote(rsend.at[me, 1 - s], rrecv.at[s, me], rss, rsr.at[0], other).start()
+    rrecv[s, me] = rsend[me, s]
+
+    swap.wait_recv()
+    theirs = frecv[...].astype(F32)
+    totals = [jnp.zeros((16, HEAD), F32), jnp.zeros((16, HEAD), F32)]
     for g in arrival:
-        settle(rsr.at[g], rrecv.at[pl.ds(0, 15 if g == 0 else 16)])
+        settle(rsr.at[g], rrecv.at[0, pl.ds(0, 31 if g == 0 else 32)])
         zz = (z + 4 - g) % 4
-        part = rrecv[zz * 16].astype(F32)
-        for n in range(1, 16):
-            part = part + rrecv[zz * 16 + n].astype(F32)
-        total = total + part
-    turned = pltpu.roll(total, 64, 1)
-    mine = jnp.where(s == 0, total, turned)[:, :64].astype(BF16)
-    theirs = jnp.where(s == 0, turned, total)[:, :64].astype(BF16)
-    fsend[...] = theirs
-    last = remote(fsend, frecv, fs, fr, other)
-    last.start()
-    out_ref[pl.ds(s * 32, 32), :] = mine
+        for e in range(2):
+            part = rrecv[e, zz * 16].astype(F32)
+            for n in range(1, 16):
+                part = part + rrecv[e, zz * 16 + n].astype(F32)
+            totals[e] = totals[e] + part
+    for e in range(2):
+        part = jnp.concatenate([totals[e], pltpu.roll(totals[e], 64, 1)], 0)[:, :64]
+        start = jnp.where(s == e, mine, theirs)
+        out_ref[pl.ds(32 * e, 32), :] = (start + part).astype(BF16)
 
     settle(cssem, csend.at[pl.ds(0, 3)], True)
     for c in small + sends:
@@ -394,8 +405,8 @@
     settle(as1, ag1.at[pl.ds(0, 63)], True)
     settle(as2, ag2.at[pl.ds(0, 63)], True)
     settle(rss, rsend.at[pl.ds(0, 63)], True)
-    last.wait()
-    out_ref[pl.ds((1 - s) * 32, 32), :] = frecv[...]
+    settle(rss, rsend.at[0, 0], True)
+    swap.wait_send()
 
 
 def on_device(
@@ -433,8 +444,8 @@
             pltpu.VMEM((256, 256), BF16),
             pltpu.VMEM((64, 32, HEAD), BF16),
             pltpu.VMEM((16, D), BF16),
-            pltpu.VMEM((64, 32, HEAD), BF16),
-            pltpu.VMEM((64, 32, HEAD), BF16),
+            pltpu.VMEM((64, 2, 16, HEAD), BF16),
+            pltpu.VMEM((2, 64, 16, HEAD), BF16),
             pltpu.VMEM((32, 64), BF16),
             pltpu.VMEM((8, 64), F32),
             pltpu.VMEM((32, HEAD), F32),

time: 51.9 us -> 50 us (0.963)
  Pallas kernels: 50.4 us -> 48.5 us
    pallas_call x1, Pallas kernels: 50.4 us -> 48.5 us  [on_device(): pl.pallas_call(layer_kernel, out_shape=jax.ShapeDtypeStruct((64, 64), BF1...]
where the time goes in v3:
time: 50 us; the launch traced here: 49.8 us
  Pallas kernels  48.5 us (97%)
  local copies, waits for them, and re-layouts  1.32 us (3%)
    pallas_call x1, Pallas kernels, on_device(): pl.pallas_call(layer_kernel, out_shape=jax.ShapeDtypeStruct((64, 64), BF1...  48.5 us
    unnamed x1, local copies, waits for them, and re-layouts  1.32 us

profile of v3, /device:TPU:1, one launch (start us, length us, event | category | flops | bytes accessed | tf_op | source)
XLA Modules:
  0.0 49.8 jit_solution(10787804155986518287)
XLA Ops:
  0.0 48.5 %shard_map.118 = bf16[64,64]{1,0:T(8,128)(2,1)} custom-call(bf16[2,8192]{1,0:T(2,128)(2,1)} %q_hbm.1, bf16[2,1024]{1,0:T(2,128)(2,1)} %lk_hbm.1, bf16[2,1024]{1,0:T(2,128)(2,1)} %lv_hbm.1, s32[2]{0:T(128)} %len_hbm.1, bf16[64,64]{1,0:T(8,128)(2,1)} %res_hbm.1, bf16[64]{0:T(256)(128)(2,1)} %gain_hbm.1, bf16[2,1024,1024]{2,1,0:T(8,128)(2,1)} %k_hbm.1, ...), custom_call_target="tpu_custom_call" | custom-call | tf_op jit(solution)/shard_map/pallas_call | solution.py:419
  48.5 1.3 %copy.14 = bf16[64,64]{1,0:T(8,128)(2,1)} copy(bf16[64,64]{1,0:T(8,128)(2,1)} %shard_map.118) | data formatting | bytes 16384

commit v4 on v3

--- a/solution.py
+++ b/solution.py
@@ -32,7 +32,7 @@
     q_ref, lk_ref, lv_ref, len_ref, res_ref, gain1, gain_ref, insem,
     kv, vv, ow, gw, uw, dw,
     qrow, lrow, csend, crecv, ag1, perm, ag2, gnat, rsend, rrecv,
-    resin, gainin, stream, gains, fsend, frecv,
+    resin, gainin, stream, gains, gainx, gainy, fsend, frecv,
     kvsem, wsem, wssem, wrsem, smallsem, smallrs,
     cssem, crsem, gssem, grsem, as1, ar1, as2, ar2, rss, rsr, fs, fr,
     ready,
@@ -205,16 +205,11 @@
     stream[...] = halves(
         res_ref[pl.ds(s * 32, 32), :].astype(F32), resin[...].astype(F32)
     )
-    gains[me] = halves(gain_ref[...], gainin[...])
-
-    def gain_stage(j, start, count, devs):
-        part = gains.at[pl.ds(start, count)]
-        cs = []
+    gainx[x] = halves(gain_ref[...], gainin[...])
+
+    def gain_stage(j, part, devs):
         for dev in devs:
-            c = remote(part, part, gssem.at[j], grsem.at[j], dev)
-            c.start()
-            cs.append(c)
-        return cs
+            remote(part, part, gssem.at[j], grsem.at[j], dev).start()
 
     def settle(sem, ref, send=False):
         c = remote(ref, ref, sem, sem, other)
@@ -223,7 +218,7 @@
         else:
             c.wait_recv()
 
-    gain_stage(0, me, 1, lines[:3])
+    gain_stage(0, gainx.at[x], lines[:3])
     pl.semaphore_wait(ready.at[0], 9)
     for dev in lines:
         pl.semaphore_signal(ready.at[1], inc=1, device_id=dev, device_id_type=MESH)
@@ -259,7 +254,7 @@
             lax.fori_loop(0, 16, step, 0)
 
     def spread(buf, ssem, rsem, by):
-        for g in order:
+        for g in order if by == "x" else arrival:
             def step(i, carry, g=g):
                 a, b = (i // 4 + 2) % 4, (i + 2) % 4
                 if by == "x":
@@ -272,8 +267,13 @@
 
     spread(ag1, as1, ar1, "x")
 
-    settle(grsem.at[0], gains.at[pl.ds(0, 3)])
-    gain_stage(1, w * 4, 4, lines[3:6])
+    settle(grsem.at[0], gainx.at[pl.ds(0, 3)])
+    gainy[y] = jnp.concatenate([gainx[j][0:1] for j in range(4)] * 2, 0)
+    gain_stage(1, gainy.at[y], lines[3:6])
+    settle(grsem.at[1], gainy.at[pl.ds(0, 3)])
+    plane = gains.at[pl.ds(z * 16, 16)]
+    plane[...] = jnp.concatenate([gainy[j][0:4] for j in range(4)], 0)
+    gain_stage(2, plane, lines[6:9])
 
     weights[0][0].wait()
     sends[0].wait_recv()
@@ -293,9 +293,6 @@
             axis=1,
         )
         total = total + dot_nt(rows, ow[:, pl.ds(pl.multiple_of(xx * 2048, 2048), 2048)])
-        if n == 1:
-            settle(grsem.at[1], gains.at[pl.ds(0, 12)])
-            gain_stage(2, z * 16, 16, lines[6:9])
     rounded = total.astype(BF16)
     ag2[me] = rounded
 
@@ -314,12 +311,13 @@
     swap.start()
 
     settle(grsem.at[2], gains.at[pl.ds(0, 48)])
-    for t in range(32):
-        first, second = mixed(gains[2 * t], gains[2 * t + 1])
-        gnat[:, HEAD * t : HEAD * (t + 1)] = jnp.concatenate([first, first], 0).astype(BF16)
-        gnat[:, 4096 + HEAD * t : 4096 + HEAD * (t + 1)] = jnp.concatenate(
-            [second, second], 0
-        ).astype(BF16)
+    evens = gains[pl.ds(0, 32, stride=2), :]
+    odds = gains[pl.ds(1, 32, stride=2), :]
+    for e, part in enumerate(mixed(evens, odds)):
+        for t in range(32):
+            gnat[:, 4096 * e + HEAD * t : 4096 * e + HEAD * (t + 1)] = jnp.broadcast_to(
+                part[t : t + 1], (16, HEAD)
+            ).astype(BF16)
     for c, _, _ in weights[1:3]:
         c.wait()
     for c in sends[1:3]:
@@ -399,8 +397,8 @@
     settle(cssem, csend.at[pl.ds(0, 3)], True)
     for c in small + sends:
         c.wait_send()
-    settle(gssem.at[0], gains.at[pl.ds(0, 3)], True)
-    settle(gssem.at[1], gains.at[pl.ds(0, 12)], True)
+    settle(gssem.at[0], gainx.at[pl.ds(0, 3)], True)
+    settle(gssem.at[1], gainy.at[pl.ds(0, 3)], True)
     settle(gssem.at[2], gains.at[pl.ds(0, 48)], True)
     settle(as1, ag1.at[pl.ds(0, 63)], True)
     settle(as2, ag2.at[pl.ds(0, 63)], True)
@@ -449,7 +447,9 @@
             pltpu.VMEM((32, 64), BF16),
             pltpu.VMEM((8, 64), F32),
             pltpu.VMEM((32, HEAD), F32),
-            pltpu.VMEM((64, 8, HEAD), F32),
+            pltpu.VMEM((64, HEAD), F32),
+            pltpu.VMEM((4, 8, HEAD), F32),
+            pltpu.VMEM((4, 8, HEAD), F32),
             pltpu.VMEM((32, 64), BF16),
             pltpu.VMEM((32, 64), BF16),
             dma((4,)), dma((4,)), dma((4,)), dma((4,)), dma((2,)), dma((2,)),

time: 50 us -> 48.9 us (0.978)
  Pallas kernels: 48.5 us -> 47.4 us
    pallas_call x1, Pallas kernels: 48.5 us -> 47.4 us  [on_device(): pl.pallas_call(layer_kernel, out_shape=jax.ShapeDtypeStruct((64, 64), BF1...]
where the time goes in v4:
time: 48.9 us; the launch traced here: 48.7 us
  Pallas kernels  47.4 us (97%)
  local copies, waits for them, and re-layouts  1.32 us (3%)
    pallas_call x1, Pallas kernels, on_device(): pl.pallas_call(layer_kernel, out_shape=jax.ShapeDtypeStruct((64, 64), BF1...  47.4 us
    unnamed x1, local copies, waits for them, and re-layouts  1.32 us

profile of v4, /device:TPU:1, one launch (start us, length us, event | category | flops | bytes accessed | tf_op | source)
XLA Modules:
  0.0 48.7 jit_solution(4211495637583709126)
XLA Ops:
  0.0 47.4 %shard_map.118 = bf16[64,64]{1,0:T(8,128)(2,1)} custom-call(bf16[2,8192]{1,0:T(2,128)(2,1)} %q_hbm.1, bf16[2,1024]{1,0:T(2,128)(2,1)} %lk_hbm.1, bf16[2,1024]{1,0:T(2,128)(2,1)} %lv_hbm.1, s32[2]{0:T(128)} %len_hbm.1, bf16[64,64]{1,0:T(8,128)(2,1)} %res_hbm.1, bf16[64]{0:T(256)(128)(2,1)} %gain_hbm.1, bf16[2,1024,1024]{2,1,0:T(8,128)(2,1)} %k_hbm.1, ...), custom_call_target="tpu_custom_call" | custom-call | tf_op jit(solution)/shard_map/pallas_call | solution.py:417
  47.4 1.3 %copy.14 = bf16[64,64]{1,0:T(8,128)(2,1)} copy(bf16[64,64]{1,0:T(8,128)(2,1)} %shard_map.118) | data formatting | bytes 16384

commit v5 on v4

--- a/solution.py
+++ b/solution.py
@@ -243,7 +243,7 @@
 
     pl.semaphore_wait(ready.at[1], 9)
 
-    order = (0, 2, 1, 3)
+    order = (0, 1, 3, 2)
     arrival = (0, 1, 3, 2)
 
     def each(g, step):

time: 48.9 us -> 46.5 us (0.951)
  Pallas kernels: 47.4 us -> 45 us
    pallas_call x1, Pallas kernels: 47.4 us -> 45 us  [on_device(): pl.pallas_call(layer_kernel, out_shape=jax.ShapeDtypeStruct((64, 64), BF1...]
where the time goes in v5:
time: 46.5 us; the launch traced here: 46.4 us
  Pallas kernels  45 us (97%)
  local copies, waits for them, and re-layouts  1.32 us (3%)
    pallas_call x1, Pallas kernels, on_device(): pl.pallas_call(layer_kernel, out_shape=jax.ShapeDtypeStruct((64, 64), BF1...  45 us
    unnamed x1, local copies, waits for them, and re-layouts  1.32 us

profile of v5, /device:TPU:1, one launch (start us, length us, event | category | flops | bytes accessed | tf_op | source)
XLA Modules:
  0.0 46.4 jit_solution(17034724072913370842)
XLA Ops:
  0.0 45.0 %shard_map.118 = bf16[64,64]{1,0:T(8,128)(2,1)} custom-call(bf16[2,8192]{1,0:T(2,128)(2,1)} %q_hbm.1, bf16[2,1024]{1,0:T(2,128)(2,1)} %lk_hbm.1, bf16[2,1024]{1,0:T(2,128)(2,1)} %lv_hbm.1, s32[2]{0:T(128)} %len_hbm.1, bf16[64,64]{1,0:T(8,128)(2,1)} %res_hbm.1, bf16[64]{0:T(256)(128)(2,1)} %gain_hbm.1, bf16[2,1024,1024]{2,1,0:T(8,128)(2,1)} %k_hbm.1, ...), custom_call_target="tpu_custom_call" | custom-call | tf_op jit(solution)/shard_map/pallas_call | solution.py:417
  45.0 1.3 %copy.14 = bf16[64,64]{1,0:T(8,128)(2,1)} copy(bf16[64,64]{1,0:T(8,128)(2,1)} %shard_map.118) | data formatting | bytes 16384
